TPU v7x, 32 devices: a whole 2x2x4 slice. The times are simulated.
32 devices in a mesh: dp: 8 (over z, y), mp: 4 (over x, core).
Axes of the slice: x: 2, y: 2, z: 4, core: 2. Of those that a mesh axis runs over, the one named last changes fastest.
Arguments:
- clean_latent: float32 [16, 768, 20], P('dp', 'mp'), may hold values from -6 to 6
- noise_draw: float32 [16, 768, 20], P('dp', 'mp'), may hold values from -6 to 6
- captions: bfloat16 [16, 256, 768], P('dp'), may hold values from -6 to 6
- caption_len: int32 [16], P('dp'), may hold values from 5 to 256, as said below
- timestep: int32 [16], P('dp'), may hold values from 0 to 999
- step_weight: float32 [1000], replicated, may hold values from 0.25 to 4
- step_count: int32 [1], replicated, may hold values from 2 to 20
- unit_slot: int32 [26], replicated, may hold values from 0 to 39, as said below
- master: float32 [40, 768, 768], P('dp', 'mp'), may hold values from -0.21875 to 0.21875
- first_moment: float32 [40, 768, 768], P('dp', 'mp'), may hold values from -8.34465e-07 to 8.34465e-07
- second_moment: float32 [40, 768, 768], P('dp', 'mp'), may hold values from 2.6031255e-16 to 1.0412502e-15
- latent_master: float32 [2, 20, 768], replicated, may hold values from -0.21875 to 0.21875
- latent_first: float32 [2, 20, 768], replicated, may hold values from -4.7683716e-06 to 4.7683716e-06
- latent_second: float32 [2, 20, 768], replicated, may hold values from 9.300595e-15 to 3.720238e-14
Outputs:
- updated_master: float32 [40, 768, 768], P('dp', 'mp')
- updated_first: float32 [40, 768, 768], P('dp', 'mp')
- updated_second: float32 [40, 768, 768], P('dp', 'mp')
- latent_updated: float32 [2, 20, 768], replicated
- latent_first_out: float32 [2, 20, 768], replicated
- latent_second_out: float32 [2, 20, 768], replicated
- grad_norm: float32 [], replicated
- loss_value: float32 [], replicated
Inputs may be any that keep to these rules, and one draw needn't show every extreme that they name: Clip b's caption occupies its first caption_len[b] token slots; some clip uses all 256. All entries differ, so every place holds at most one matrix; matrix u is owned by dp index unit_slot[u] // 5 in its place unit_slot[u] % 5; some dp index owns 5 matrices, every other index owns 0 to 5.
All inputs are finite; a program needn't handle non-finite values.
Results may differ from a plain program's by a relative error of at most 0.017.
Values may be sent and summed in bfloat16 or wider, within the bound.
No kernel may reach another device: no remote copies, remote signals or barrier semaphores. Data moves between devices by JAX's collectives and lax.ppermute only.
A program may use at most 192 MiB of HBM per device.

v0:
```python
import math
import jax
import jax.numpy as jnp
from jax import lax
from jax.sharding import PartitionSpec as P

D = 768
HD = 64
C = 20
FRAMES = 768
NT = 1000
UNITS = 26
highest = lax.Precision.HIGHEST
beta_first = 0.9
beta_second = 0.999
adam_epsilon = 1e-08
learn_rate = 0.02
decay_rate = 0.1
clip_limit = 0.002
norm_epsilon = 1e-06
masked_score = -1e30
bfloat = jnp.bfloat16
single = jnp.float32


def broadcast(array, axis, root):
    mine = lax.axis_index(axis) == root
    return lax.psum(jnp.where(mine, array, jnp.zeros_like(array)), axis)


def normed(values):
    center = values - jnp.mean(values, axis=-1, keepdims=True)
    spread_sq = jnp.mean(center * center, axis=-1, keepdims=True)
    return center * lax.rsqrt(spread_sq + norm_epsilon)


def modulate(values, shift, scale):
    return normed(values) * (1.0 + scale[:, None, :]) + shift[:, None, :]


def modulate_back(values, shift, scale, grad):
    _, pullback = jax.vjp(modulate, values, shift, scale)
    return pullback(grad)


def adamw(weight, moment, square, grad, count):
    moment = beta_first * moment + (1.0 - beta_first) * grad
    square = beta_second * square + (1.0 - beta_second) * grad * grad
    first_fix = 1.0 - jnp.power(beta_first, count)
    second_fix = 1.0 - jnp.power(beta_second, count)
    update = (
        moment / first_fix / (jnp.sqrt(square / second_fix) + adam_epsilon) + decay_rate * weight
    )
    return (weight - learn_rate * update, moment, square)


def sinusoid(timestep):
    half_width = D // 2
    frequency = jnp.exp(-math.log(10000.0) * jnp.arange(half_width).astype(single) / half_width)
    angles = timestep.astype(single)[:, None] * frequency[None, :]
    return jnp.concatenate([jnp.cos(angles), jnp.sin(angles)], axis=1)


def matmul(form, left, right):
    return jnp.einsum(form, left, right, preferred_element_type=single)


def masked_scores(query, keys, mask):
    scores = matmul("fhk,ghk->hfg", query, keys) * HD ** (-0.5)
    return jnp.where(mask[None, None, :], scores, masked_score)


def attend_forward(parts):
    query, keys, values, mask = parts
    scores = masked_scores(query, keys, mask)
    row_max = jnp.max(scores, axis=-1, keepdims=True)
    shifted = jnp.exp(scores - row_max)
    row_total = jnp.sum(shifted, axis=-1, keepdims=True)
    probs = shifted / row_total
    output = matmul("hfg,ghk->fhk", probs.astype(bfloat), values)
    return (output.astype(bfloat), (row_max + jnp.log(row_total))[..., 0])


def attend_backward(parts):
    query, keys, values, mask, grad_out, log_total = parts
    probs = jnp.exp(masked_scores(query, keys, mask) - log_total[..., None])
    grad_probs = matmul("fhk,ghk->hfg", grad_out, values)
    inner = jnp.sum(probs * grad_probs, axis=-1, keepdims=True)
    grad_scores = (probs * (grad_probs - inner)).astype(bfloat)
    grad_query = matmul("hfg,ghk->fhk", grad_scores, keys) * HD ** (-0.5)
    grad_keys = matmul("hfg,fhk->ghk", grad_scores, query) * HD ** (-0.5)
    grad_values = matmul("hfg,fhk->ghk", probs.astype(bfloat), grad_out)
    return (grad_query.astype(bfloat), grad_keys.astype(bfloat), grad_values.astype(bfloat))


def split_heads(values):
    return values.reshape(values.shape[0], values.shape[1], -1, HD)


def merge_heads(values):
    return values.reshape(values.shape[0], values.shape[1], -1)


def attention(query, keys, values, mask):
    output, log_total = lax.map(
        attend_forward, (split_heads(query), split_heads(keys), split_heads(values), mask)
    )
    return (merge_heads(output), log_total)


def attention_back(query, keys, values, mask, grad_out, log_total):
    grads = lax.map(
        attend_backward,
        (
            split_heads(query),
            split_heads(keys),
            split_heads(values),
            mask,
            split_heads(grad_out),
            log_total,
        ),
    )
    return tuple((merge_heads(item) for item in grads))


def spread(values):
    return lax.all_gather(values, "mp", axis=1, tiled=True)


def collect(values):
    return lax.psum_scatter(
        values.astype(jnp.bfloat16), "mp", scatter_dimension=1, tiled=True
    ).astype(jnp.float32)


def side_by_side(stack):
    return jnp.transpose(stack, (1, 0, 2)).reshape(stack.shape[1], -1)


def body(
    clean_latent,
    noise_draw,
    captions,
    caption_len,
    timestep,
    step_weight,
    step_count,
    unit_slot,
    master,
    first_moment,
    second_moment,
    latent_master,
    latent_first,
    latent_second,
):
    slots = master.shape[0]
    owner = unit_slot // slots
    place = unit_slot % slots

    def fetch_one(running, index):
        local = lax.dynamic_index_in_dim(master, place[index], 0, keepdims=False).astype(bfloat)
        return (running, broadcast(local, "dp", owner[index]))

    _, fetched = lax.scan(fetch_one, 0, jnp.arange(UNITS))
    weights = jnp.swapaxes(fetched, 1, 2)
    width = weights.shape[2]
    table = jnp.arange(step_weight.shape[0])
    clip_weight = jnp.sum(
        jnp.where(timestep[:, None] == table[None, :], step_weight[None, :], 0.0), axis=1
    )
    weight_total = lax.psum(jnp.sum(clip_weight), "dp")
    level = (timestep.astype(single) + 0.5) / NT
    noisy = (1.0 - level)[:, None, None] * clean_latent + level[:, None, None] * noise_draw
    target = noise_draw - clean_latent
    cap_mask = jnp.arange(captions.shape[1])[None, :] < caption_len[:, None]
    pooled = (
        jnp.sum(jnp.where(cap_mask[:, :, None], captions.astype(single), 0.0), axis=1)
        / caption_len.astype(single)[:, None]
    )
    sinus_low = sinusoid(timestep).astype(bfloat)
    pooled_low = pooled.astype(bfloat)
    cond_part = matmul("bd,de->be", sinus_low, weights[24]) + matmul(
        "bd,de->be", pooled_low, weights[25]
    )
    cond = lax.all_gather(cond_part, "mp", axis=1, tiled=True)
    active = jax.nn.silu(cond).astype(bfloat)
    modulation = lax.all_gather(
        matmul("bd,jde->bje", active, weights[16:24]), "mp", axis=2, tiled=True
    )
    hidden_zero = jnp.einsum("bfc,cd->bfd", noisy, latent_master[0], precision=highest)
    w_attn = side_by_side(weights[0:3])
    first_in = spread(modulate(hidden_zero, modulation[:, 0], modulation[:, 1]).astype(bfloat))
    self_proj = matmul("bfd,de->bfe", first_in, w_attn).astype(bfloat)
    self_query, self_keys, self_values = jnp.split(self_proj, 3, axis=2)
    self_mask = jnp.ones((self_query.shape[0], self_query.shape[1]), bool)
    self_flat, self_total = attention(self_query, self_keys, self_values, self_mask)
    self_branch = collect(matmul("bfk,dk->bfd", self_flat, weights[3]))
    hidden_one = hidden_zero + modulation[:, 2, None, :] * self_branch
    second_in = spread(normed(hidden_one).astype(bfloat))
    cross_query = matmul("bfd,de->bfe", second_in, weights[4]).astype(bfloat)
    w_text = side_by_side(weights[5:7])
    cross_keys, cross_values = jnp.split(
        matmul("bld,de->ble", captions, w_text).astype(bfloat), 2, axis=2
    )
    cross_flat, cross_total = attention(cross_query, cross_keys, cross_values, cap_mask)
    cross_branch = collect(matmul("bfk,dk->bfd", cross_flat, weights[7]))
    hidden_two = hidden_one + cross_branch
    w_up = side_by_side(weights[8:12])
    w_down = side_by_side(weights[12:16])
    third_in = spread(modulate(hidden_two, modulation[:, 3], modulation[:, 4]).astype(bfloat))
    upper_wide = matmul("bfd,dk->bfk", third_in, w_up).astype(bfloat).astype(single)
    activated = jax.nn.gelu(upper_wide, approximate=True).astype(bfloat)
    mlp_branch = collect(matmul("bfk,dk->bfd", activated, w_down))
    hidden_three = hidden_two + modulation[:, 5, None, :] * mlp_branch
    final_wide = (
        modulate(hidden_three, modulation[:, 6], modulation[:, 7]).astype(bfloat).astype(single)
    )
    predicted = jnp.einsum("bfd,cd->bfc", final_wide, latent_master[1], precision=highest)
    error = predicted - target
    loss_local = jnp.sum(clip_weight[:, None, None] * error * error)
    grad_pred = 2.0 / (C * FRAMES) * clip_weight[:, None, None] * error / weight_total
    grad_out_proj = jnp.einsum("bfc,bfd->cd", grad_pred, final_wide, precision=highest)
    grad_final = jnp.einsum("bfc,cd->bfd", grad_pred, latent_master[1], precision=highest)
    grad_three, shift_f, scale_f = modulate_back(
        hidden_three, modulation[:, 6], modulation[:, 7], grad_final
    )
    gate_m_grad = jnp.sum(grad_three * mlp_branch, axis=1)
    grad_mlp = spread((modulation[:, 5, None, :] * grad_three).astype(bfloat))
    grad_act = matmul("bfd,dk->bfk", grad_mlp, w_down)
    grad_w_down = matmul("bfd,bfk->dk", grad_mlp, activated)
    _, gelu_back = jax.vjp(lambda inner_in: jax.nn.gelu(inner_in, approximate=True), upper_wide)
    grad_upper = gelu_back(grad_act)[0].astype(bfloat)
    grad_w_up = matmul("bfd,bfk->dk", third_in, grad_upper)
    grad_third = collect(matmul("bfk,dk->bfd", grad_upper, w_up))
    grad_two, shift_m, scale_m = modulate_back(
        hidden_two, modulation[:, 3], modulation[:, 4], grad_third
    )
    grad_two = grad_two + grad_three
    grad_cross = spread(grad_two.astype(bfloat))
    grad_cross_flat = matmul("bfd,dk->bfk", grad_cross, weights[7]).astype(bfloat)
    grad_w_cross_out = matmul("bfd,bfk->dk", grad_cross, cross_flat)
    cq_grad, ck_grad, cv_grad = attention_back(
        cross_query, cross_keys, cross_values, cap_mask, grad_cross_flat, cross_total
    )
    grad_w_cq = matmul("bfd,bfk->dk", second_in, cq_grad)
    grad_w_text = matmul("bld,ble->de", captions, jnp.concatenate([ck_grad, cv_grad], axis=2))
    grad_second = collect(matmul("bfk,dk->bfd", cq_grad, weights[4]))
    _, norm_back = jax.vjp(normed, hidden_one)
    grad_one = grad_two + norm_back(grad_second)[0]
    gate_a_grad = jnp.sum(grad_one * self_branch, axis=1)
    grad_self = spread((modulation[:, 2, None, :] * grad_one).astype(bfloat))
    grad_self_flat = matmul("bfd,dk->bfk", grad_self, weights[3]).astype(bfloat)
    grad_w_self_out = matmul("bfd,bfk->dk", grad_self, self_flat)
    sq_grad, sk_grad, sv_grad = attention_back(
        self_query, self_keys, self_values, self_mask, grad_self_flat, self_total
    )
    grad_proj = jnp.concatenate([sq_grad, sk_grad, sv_grad], axis=2)
    grad_w_attn = matmul("bfd,bfe->de", first_in, grad_proj)
    grad_first = collect(matmul("bfe,de->bfd", grad_proj, w_attn))
    grad_zero, shift_a, scale_a = modulate_back(
        hidden_zero, modulation[:, 0], modulation[:, 1], grad_first
    )
    grad_zero = grad_zero + grad_one
    grad_in_proj = jnp.einsum("bfc,bfd->cd", noisy, grad_zero, precision=highest)
    grad_mod = jnp.stack(
        [shift_a, scale_a, gate_a_grad, shift_m, scale_m, gate_m_grad, shift_f, scale_f], axis=1
    )
    mod_own = (
        lax.psum_scatter(grad_mod.astype(jnp.bfloat16), "mp", scatter_dimension=2, tiled=True)
        .astype(jnp.float32)
        .astype(bfloat)
    )
    grad_ada = matmul("bd,bje->jde", active, mod_own)
    grad_active = matmul("bje,jde->bd", mod_own, weights[16:24])
    _, silu_back = jax.vjp(jax.nn.silu, cond)
    cond_own = lax.psum_scatter(
        silu_back(grad_active)[0], "mp", scatter_dimension=1, tiled=True
    ).astype(bfloat)
    grad_time = matmul("bd,be->de", sinus_low, cond_own)
    grad_pool = matmul("bd,be->de", pooled_low, cond_own)

    def columns(matrix, count):
        return jnp.transpose(matrix.reshape(matrix.shape[0], count, width), (1, 0, 2))

    grads_cols = jnp.concatenate(
        [
            columns(grad_w_attn, 3),
            grad_w_self_out[None],
            grad_w_cq[None],
            columns(grad_w_text, 2),
            grad_w_cross_out[None],
            columns(grad_w_up, 4),
            columns(grad_w_down, 4),
            grad_ada,
            grad_time[None],
            grad_pool[None],
        ],
        axis=0,
    )
    grads = jnp.swapaxes(grads_cols, 1, 2)
    local_ids = lax.axis_index("dp") * slots + jnp.arange(slots)
    pick = (unit_slot[None, :] == local_ids[:, None]).astype(single)
    live_slot = jnp.sum(pick, axis=1) > 0.5
    summed = lax.psum(grads, "dp")
    owned = jnp.einsum("su,ude->sde", pick, summed, precision=highest)
    latent_grad, loss_sum = lax.psum(
        (jnp.stack([grad_in_proj, grad_out_proj]), loss_local), ("dp", "mp")
    )
    square_sum = lax.psum(jnp.sum(owned * owned), ("dp", "mp")) + jnp.sum(latent_grad * latent_grad)
    grad_norm = jnp.sqrt(square_sum)
    factor = clip_limit / jnp.maximum(grad_norm, clip_limit)
    count = step_count[0].astype(single)
    new_weight, new_moment, new_square = adamw(
        master, first_moment, second_moment, owned * factor, count
    )
    keep = live_slot[:, None, None]
    latent_weight, latent_moment, latent_square = adamw(
        latent_master, latent_first, latent_second, latent_grad * factor, count
    )
    loss_value = loss_sum / (C * FRAMES * weight_total)
    return (
        jnp.where(keep, new_weight, master),
        jnp.where(keep, new_moment, first_moment),
        jnp.where(keep, new_square, second_moment),
        latent_weight,
        latent_moment,
        latent_square,
        grad_norm,
        loss_value,
    )


def solution(mesh):
    placed = (
        P("dp", "mp", None),
        P("dp", "mp", None),
        P("dp", None, None),
        P("dp"),
        P("dp"),
        P(),
        P(),
        P(),
        P("dp", "mp", None),
        P("dp", "mp", None),
        P("dp", "mp", None),
        P(),
        P(),
        P(),
    )
    return jax.shard_map(
        body,
        mesh=mesh,
        in_specs=placed,
        out_specs=(
            P("dp", "mp", None),
            P("dp", "mp", None),
            P("dp", "mp", None),
            P(),
            P(),
            P(),
            P(),
            P(),
        ),
        check_vma=False,
    )
```

profile of v0, /device:TPU:0, one launch (start us, length us, event | category | flops | bytes accessed | tf_op | source)
XLA Modules:
  0.0 3431.0 jit_solution(15511548824490936030)
XLA Ops:
  17.4 2054.4 %while.62 = (s32[]{:T(128)}, bf16[26,192,768]{2,1,0:T(8,128)(2,1)}, s32[26]{0:T(128)S(1)}, s32[26]{0:T(128)S(1)}, s32[26]{0:T(128)S(1)}, /*index=5*/bf16[5,192,7...) while((s32[]{:T(128)}, bf16[26,192,768]{2,1,0:T(8,128)(2,1)}, ...), condition=%wide.region_5.6_spmd, body=%wide.region_3.5_spmd.sunk | while | flops 294924 | bytes 2949439 | solution.py:164
  24.6 73.7 %all-reduce.9.cloned.1.call-done = bf16[1,192,768]{2,1,0:T(8,128)(2,1)} async-done(((bf16[1,192,768]{2,1,0:T(8,128)(2,1)}), bf16[1,192,768]{2,1,0:T(8,128)(2,1)}) %all-reduce.9.cloned.1.call-update) | async-done | bytes 294928 | tf_op jit(solution)/shard_map/while/body/eval_jaxpr/psum | solution.py:28
  107.0 70.1 %all-reduce.9.cloned.1.call-done = bf16[1,192,768]{2,1,0:T(8,128)(2,1)} async-done(((bf16[1,192,768]{2,1,0:T(8,128)(2,1)}), bf16[1,192,768]{2,1,0:T(8,128)(2,1)}) %all-reduce.9.cloned.1.call-update) | async-done | bytes 294928 | tf_op jit(solution)/shard_map/while/body/eval_jaxpr/psum | solution.py:28
  185.9 70.1 %all-reduce.9.cloned.1.call-done = bf16[1,192,768]{2,1,0:T(8,128)(2,1)} async-done(((bf16[1,192,768]{2,1,0:T(8,128)(2,1)}), bf16[1,192,768]{2,1,0:T(8,128)(2,1)}) %all-reduce.9.cloned.1.call-update) | async-done | bytes 294928 | tf_op jit(solution)/shard_map/while/body/eval_jaxpr/psum | solution.py:28
  264.7 70.1 %all-reduce.9.cloned.1.call-done = bf16[1,192,768]{2,1,0:T(8,128)(2,1)} async-done(((bf16[1,192,768]{2,1,0:T(8,128)(2,1)}), bf16[1,192,768]{2,1,0:T(8,128)(2,1)}) %all-reduce.9.cloned.1.call-update) | async-done | bytes 294928 | tf_op jit(solution)/shard_map/while/body/eval_jaxpr/psum | solution.py:28
  343.6 70.1 %all-reduce.9.cloned.1.call-done = bf16[1,192,768]{2,1,0:T(8,128)(2,1)} async-done(((bf16[1,192,768]{2,1,0:T(8,128)(2,1)}), bf16[1,192,768]{2,1,0:T(8,128)(2,1)}) %all-reduce.9.cloned.1.call-update) | async-done | bytes 294928 | tf_op jit(solution)/shard_map/while/body/eval_jaxpr/psum | solution.py:28
  422.5 70.1 %all-reduce.9.cloned.1.call-done = bf16[1,192,768]{2,1,0:T(8,128)(2,1)} async-done(((bf16[1,192,768]{2,1,0:T(8,128)(2,1)}), bf16[1,192,768]{2,1,0:T(8,128)(2,1)}) %all-reduce.9.cloned.1.call-update) | async-done | bytes 294928 | tf_op jit(solution)/shard_map/while/body/eval_jaxpr/psum | solution.py:28
  501.3 70.1 %all-reduce.9.cloned.1.call-done = bf16[1,192,768]{2,1,0:T(8,128)(2,1)} async-done(((bf16[1,192,768]{2,1,0:T(8,128)(2,1)}), bf16[1,192,768]{2,1,0:T(8,128)(2,1)}) %all-reduce.9.cloned.1.call-update) | async-done | bytes 294928 | tf_op jit(solution)/shard_map/while/body/eval_jaxpr/psum | solution.py:28
  580.2 70.1 %all-reduce.9.cloned.1.call-done = bf16[1,192,768]{2,1,0:T(8,128)(2,1)} async-done(((bf16[1,192,768]{2,1,0:T(8,128)(2,1)}), bf16[1,192,768]{2,1,0:T(8,128)(2,1)}) %all-reduce.9.cloned.1.call-update) | async-done | bytes 294928 | tf_op jit(solution)/shard_map/while/body/eval_jaxpr/psum | solution.py:28
  659.1 70.1 %all-reduce.9.cloned.1.call-done = bf16[1,192,768]{2,1,0:T(8,128)(2,1)} async-done(((bf16[1,192,768]{2,1,0:T(8,128)(2,1)}), bf16[1,192,768]{2,1,0:T(8,128)(2,1)}) %all-reduce.9.cloned.1.call-update) | async-done | bytes 294928 | tf_op jit(solution)/shard_map/while/body/eval_jaxpr/psum | solution.py:28
  738.0 70.1 %all-reduce.9.cloned.1.call-done = bf16[1,192,768]{2,1,0:T(8,128)(2,1)} async-done(((bf16[1,192,768]{2,1,0:T(8,128)(2,1)}), bf16[1,192,768]{2,1,0:T(8,128)(2,1)}) %all-reduce.9.cloned.1.call-update) | async-done | bytes 294928 | tf_op jit(solution)/shard_map/while/body/eval_jaxpr/psum | solution.py:28
  816.9 70.1 %all-reduce.9.cloned.1.call-done = bf16[1,192,768]{2,1,0:T(8,128)(2,1)} async-done(((bf16[1,192,768]{2,1,0:T(8,128)(2,1)}), bf16[1,192,768]{2,1,0:T(8,128)(2,1)}) %all-reduce.9.cloned.1.call-update) | async-done | bytes 294928 | tf_op jit(solution)/shard_map/while/body/eval_jaxpr/psum | solution.py:28
  895.7 70.1 %all-reduce.9.cloned.1.call-done = bf16[1,192,768]{2,1,0:T(8,128)(2,1)} async-done(((bf16[1,192,768]{2,1,0:T(8,128)(2,1)}), bf16[1,192,768]{2,1,0:T(8,128)(2,1)}) %all-reduce.9.cloned.1.call-update) | async-done | bytes 294928 | tf_op jit(solution)/shard_map/while/body/eval_jaxpr/psum | solution.py:28
  974.6 70.1 %all-reduce.9.cloned.1.call-done = bf16[1,192,768]{2,1,0:T(8,128)(2,1)} async-done(((bf16[1,192,768]{2,1,0:T(8,128)(2,1)}), bf16[1,192,768]{2,1,0:T(8,128)(2,1)}) %all-reduce.9.cloned.1.call-update) | async-done | bytes 294928 | tf_op jit(solution)/shard_map/while/body/eval_jaxpr/psum | solution.py:28
  1053.4 70.1 %all-reduce.9.cloned.1.call-done = bf16[1,192,768]{2,1,0:T(8,128)(2,1)} async-done(((bf16[1,192,768]{2,1,0:T(8,128)(2,1)}), bf16[1,192,768]{2,1,0:T(8,128)(2,1)}) %all-reduce.9.cloned.1.call-update) | async-done | bytes 294928 | tf_op jit(solution)/shard_map/while/body/eval_jaxpr/psum | solution.py:28
  1132.3 70.1 %all-reduce.9.cloned.1.call-done = bf16[1,192,768]{2,1,0:T(8,128)(2,1)} async-done(((bf16[1,192,768]{2,1,0:T(8,128)(2,1)}), bf16[1,192,768]{2,1,0:T(8,128)(2,1)}) %all-reduce.9.cloned.1.call-update) | async-done | bytes 294928 | tf_op jit(solution)/shard_map/while/body/eval_jaxpr/psum | solution.py:28
  1211.2 70.1 %all-reduce.9.cloned.1.call-done = bf16[1,192,768]{2,1,0:T(8,128)(2,1)} async-done(((bf16[1,192,768]{2,1,0:T(8,128)(2,1)}), bf16[1,192,768]{2,1,0:T(8,128)(2,1)}) %all-reduce.9.cloned.1.call-update) | async-done | bytes 294928 | tf_op jit(solution)/shard_map/while/body/eval_jaxpr/psum | solution.py:28
  1290.1 70.1 %all-reduce.9.cloned.1.call-done = bf16[1,192,768]{2,1,0:T(8,128)(2,1)} async-done(((bf16[1,192,768]{2,1,0:T(8,128)(2,1)}), bf16[1,192,768]{2,1,0:T(8,128)(2,1)}) %all-reduce.9.cloned.1.call-update) | async-done | bytes 294928 | tf_op jit(solution)/shard_map/while/body/eval_jaxpr/psum | solution.py:28
  1369.0 70.1 %all-reduce.9.cloned.1.call-done = bf16[1,192,768]{2,1,0:T(8,128)(2,1)} async-done(((bf16[1,192,768]{2,1,0:T(8,128)(2,1)}), bf16[1,192,768]{2,1,0:T(8,128)(2,1)}) %all-reduce.9.cloned.1.call-update) | async-done | bytes 294928 | tf_op jit(solution)/shard_map/while/body/eval_jaxpr/psum | solution.py:28
  1447.9 70.1 %all-reduce.9.cloned.1.call-done = bf16[1,192,768]{2,1,0:T(8,128)(2,1)} async-done(((bf16[1,192,768]{2,1,0:T(8,128)(2,1)}), bf16[1,192,768]{2,1,0:T(8,128)(2,1)}) %all-reduce.9.cloned.1.call-update) | async-done | bytes 294928 | tf_op jit(solution)/shard_map/while/body/eval_jaxpr/psum | solution.py:28
  1526.7 70.1 %all-reduce.9.cloned.1.call-done = bf16[1,192,768]{2,1,0:T(8,128)(2,1)} async-done(((bf16[1,192,768]{2,1,0:T(8,128)(2,1)}), bf16[1,192,768]{2,1,0:T(8,128)(2,1)}) %all-reduce.9.cloned.1.call-update) | async-done | bytes 294928 | tf_op jit(solution)/shard_map/while/body/eval_jaxpr/psum | solution.py:28
  1605.6 70.1 %all-reduce.9.cloned.1.call-done = bf16[1,192,768]{2,1,0:T(8,128)(2,1)} async-done(((bf16[1,192,768]{2,1,0:T(8,128)(2,1)}), bf16[1,192,768]{2,1,0:T(8,128)(2,1)}) %all-reduce.9.cloned.1.call-update) | async-done | bytes 294928 | tf_op jit(solution)/shard_map/while/body/eval_jaxpr/psum | solution.py:28
  1684.5 70.1 %all-reduce.9.cloned.1.call-done = bf16[1,192,768]{2,1,0:T(8,128)(2,1)} async-done(((bf16[1,192,768]{2,1,0:T(8,128)(2,1)}), bf16[1,192,768]{2,1,0:T(8,128)(2,1)}) %all-reduce.9.cloned.1.call-update) | async-done | bytes 294928 | tf_op jit(solution)/shard_map/while/body/eval_jaxpr/psum | solution.py:28
  1763.4 70.1 %all-reduce.9.cloned.1.call-done = bf16[1,192,768]{2,1,0:T(8,128)(2,1)} async-done(((bf16[1,192,768]{2,1,0:T(8,128)(2,1)}), bf16[1,192,768]{2,1,0:T(8,128)(2,1)}) %all-reduce.9.cloned.1.call-update) | async-done | bytes 294928 | tf_op jit(solution)/shard_map/while/body/eval_jaxpr/psum | solution.py:28
  1842.2 70.1 %all-reduce.9.cloned.1.call-done = bf16[1,192,768]{2,1,0:T(8,128)(2,1)} async-done(((bf16[1,192,768]{2,1,0:T(8,128)(2,1)}), bf16[1,192,768]{2,1,0:T(8,128)(2,1)}) %all-reduce.9.cloned.1.call-update) | async-done | bytes 294928 | tf_op jit(solution)/shard_map/while/body/eval_jaxpr/psum | solution.py:28
  1921.1 70.1 %all-reduce.9.cloned.1.call-done = bf16[1,192,768]{2,1,0:T(8,128)(2,1)} async-done(((bf16[1,192,768]{2,1,0:T(8,128)(2,1)}), bf16[1,192,768]{2,1,0:T(8,128)(2,1)}) %all-reduce.9.cloned.1.call-update) | async-done | bytes 294928 | tf_op jit(solution)/shard_map/while/body/eval_jaxpr/psum | solution.py:28
  2000.0 70.1 %all-reduce.9.cloned.1.call-done = bf16[1,192,768]{2,1,0:T(8,128)(2,1)} async-done(((bf16[1,192,768]{2,1,0:T(8,128)(2,1)}), bf16[1,192,768]{2,1,0:T(8,128)(2,1)}) %all-reduce.9.cloned.1.call-update) | async-done | bytes 294928 | tf_op jit(solution)/shard_map/while/body/eval_jaxpr/psum | solution.py:28
  2449.1 33.0 reduce-scatter.21.cloned.1.call-done
  2646.2 46.0 %concatenate.16 = f32[26,768,192]{1,0,2:T(8,128)} concatenate(f32[3,768,192]{1,0,2:T(4,128)S(1)} %bitcast.450, f32[1,768,192]{1,0,2:T(1,128)} %copy.315, f32[1,768,192]{1,0,2:T(1,128)} %copy.316, f32[2,768,192]{1,0,2:T(2,128)S(1)} %bitcast.466, f32[1,768,192]{1,0,2:T(1,128)} %copy.317, f32[4,768,192]{1,0,2:T(4,128)} %get-tuple-element.415, f32[4,768,192]{1,0,2:T(4,128)} %get-tuple-element.414, ...), dimensions={0} | concatenate | bytes 30670848 | tf_op jit(solution)/shard_map/concatenate | solution.py:285
  2693.8 73.2 %all-reduce.7.cloned.1.call-done = f32[2,20,768]{2,1,0:T(8,128)} async-done(((f32[2,20,768]{2,1,0:T(8,128)}), f32[2,20,768]{2,1,0:T(8,128)}) %all-reduce.7.cloned.1.call-update) | async-done | bytes 122896 | tf_op jit(solution)/shard_map/psum | solution.py:306
  2768.6 571.5 %all-reduce.5.cloned.1.call-done = f32[26,192,768]{2,0,1:T(8,128)} async-done(((f32[26,192,768]{2,0,1:T(8,128)}), f32[26,192,768]{2,0,1:T(8,128)}) %all-reduce.5.cloned.1.call-update) | async-done | bytes 15335440 | tf_op jit(solution)/shard_map/psum | solution.py:304
  3352.7 39.8 %all-reduce = (f32[]{:T(128)}, f32[]{:T(128)}) all-reduce(f32[]{:T(128)} %get-tuple-element.410, f32[]{:T(128)} %get-tuple-element.412), channel_id=1, replica_groups=mesh['dp'=8,'mp'=4] {'dp','mp'}, use_global_device_ids=true, to_apply=%region_54.55 | all-reduce | flops 2 | bytes 16 | tf_op jit(solution)/shard_map/psum | solution.py:309
  (707 shorter events, 759.0 us)
Async XLA Ops:
  17.4 80.8 %all-reduce.9.cloned.1.call-start = ((), (), s32[]{:S(2)}) async-start(), calls=%async_computation.24 | async-start | bytes 589824 | tf_op jit(solution)/shard_map/while/body/eval_jaxpr/psum | solution.py:28
  99.9 77.2 %all-reduce.9.cloned.1.call-start = ((), (), s32[]{:S(2)}) async-start(), calls=%async_computation.24 | async-start | bytes 589824 | tf_op jit(solution)/shard_map/while/body/eval_jaxpr/psum | solution.py:28
  178.8 77.2 %all-reduce.9.cloned.1.call-start = ((), (), s32[]{:S(2)}) async-start(), calls=%async_computation.24 | async-start | bytes 589824 | tf_op jit(solution)/shard_map/while/body/eval_jaxpr/psum | solution.py:28
  257.7 77.2 %all-reduce.9.cloned.1.call-start = ((), (), s32[]{:S(2)}) async-start(), calls=%async_computation.24 | async-start | bytes 589824 | tf_op jit(solution)/shard_map/while/body/eval_jaxpr/psum | solution.py:28
  336.5 77.2 %all-reduce.9.cloned.1.call-start = ((), (), s32[]{:S(2)}) async-start(), calls=%async_computation.24 | async-start | bytes 589824 | tf_op jit(solution)/shard_map/while/body/eval_jaxpr/psum | solution.py:28
  415.4 77.2 %all-reduce.9.cloned.1.call-start = ((), (), s32[]{:S(2)}) async-start(), calls=%async_computation.24 | async-start | bytes 589824 | tf_op jit(solution)/shard_map/while/body/eval_jaxpr/psum | solution.py:28
  494.3 77.2 %all-reduce.9.cloned.1.call-start = ((), (), s32[]{:S(2)}) async-start(), calls=%async_computation.24 | async-start | bytes 589824 | tf_op jit(solution)/shard_map/while/body/eval_jaxpr/psum | solution.py:28
  573.2 77.2 %all-reduce.9.cloned.1.call-start = ((), (), s32[]{:S(2)}) async-start(), calls=%async_computation.24 | async-start | bytes 589824 | tf_op jit(solution)/shard_map/while/body/eval_jaxpr/psum | solution.py:28
  652.0 77.2 %all-reduce.9.cloned.1.call-start = ((), (), s32[]{:S(2)}) async-start(), calls=%async_computation.24 | async-start | bytes 589824 | tf_op jit(solution)/shard_map/while/body/eval_jaxpr/psum | solution.py:28
  730.9 77.2 %all-reduce.9.cloned.1.call-start = ((), (), s32[]{:S(2)}) async-start(), calls=%async_computation.24 | async-start | bytes 589824 | tf_op jit(solution)/shard_map/while/body/eval_jaxpr/psum | solution.py:28
  809.8 77.2 %all-reduce.9.cloned.1.call-start = ((), (), s32[]{:S(2)}) async-start(), calls=%async_computation.24 | async-start | bytes 589824 | tf_op jit(solution)/shard_map/while/body/eval_jaxpr/psum | solution.py:28
  888.7 77.2 %all-reduce.9.cloned.1.call-start = ((), (), s32[]{:S(2)}) async-start(), calls=%async_computation.24 | async-start | bytes 589824 | tf_op jit(solution)/shard_map/while/body/eval_jaxpr/psum | solution.py:28
  967.5 77.2 %all-reduce.9.cloned.1.call-start = ((), (), s32[]{:S(2)}) async-start(), calls=%async_computation.24 | async-start | bytes 589824 | tf_op jit(solution)/shard_map/while/body/eval_jaxpr/psum | solution.py:28
  1046.4 77.2 %all-reduce.9.cloned.1.call-start = ((), (), s32[]{:S(2)}) async-start(), calls=%async_computation.24 | async-start | bytes 589824 | tf_op jit(solution)/shard_map/while/body/eval_jaxpr/psum | solution.py:28
  1125.3 77.2 %all-reduce.9.cloned.1.call-start = ((), (), s32[]{:S(2)}) async-start(), calls=%async_computation.24 | async-start | bytes 589824 | tf_op jit(solution)/shard_map/while/body/eval_jaxpr/psum | solution.py:28
  1204.1 77.2 %all-reduce.9.cloned.1.call-start = ((), (), s32[]{:S(2)}) async-start(), calls=%async_computation.24 | async-start | bytes 589824 | tf_op jit(solution)/shard_map/while/body/eval_jaxpr/psum | solution.py:28
  1283.0 77.2 %all-reduce.9.cloned.1.call-start = ((), (), s32[]{:S(2)}) async-start(), calls=%async_computation.24 | async-start | bytes 589824 | tf_op jit(solution)/shard_map/while/body/eval_jaxpr/psum | solution.py:28
  1361.9 77.2 %all-reduce.9.cloned.1.call-start = ((), (), s32[]{:S(2)}) async-start(), calls=%async_computation.24 | async-start | bytes 589824 | tf_op jit(solution)/shard_map/while/body/eval_jaxpr/psum | solution.py:28
  1440.8 77.2 %all-reduce.9.cloned.1.call-start = ((), (), s32[]{:S(2)}) async-start(), calls=%async_computation.24 | async-start | bytes 589824 | tf_op jit(solution)/shard_map/while/body/eval_jaxpr/psum | solution.py:28
  1519.7 77.2 %all-reduce.9.cloned.1.call-start = ((), (), s32[]{:S(2)}) async-start(), calls=%async_computation.24 | async-start | bytes 589824 | tf_op jit(solution)/shard_map/while/body/eval_jaxpr/psum | solution.py:28
  1598.5 77.2 %all-reduce.9.cloned.1.call-start = ((), (), s32[]{:S(2)}) async-start(), calls=%async_computation.24 | async-start | bytes 589824 | tf_op jit(solution)/shard_map/while/body/eval_jaxpr/psum | solution.py:28
  1677.4 77.2 %all-reduce.9.cloned.1.call-start = ((), (), s32[]{:S(2)}) async-start(), calls=%async_computation.24 | async-start | bytes 589824 | tf_op jit(solution)/shard_map/while/body/eval_jaxpr/psum | solution.py:28
  1756.3 77.2 %all-reduce.9.cloned.1.call-start = ((), (), s32[]{:S(2)}) async-start(), calls=%async_computation.24 | async-start | bytes 589824 | tf_op jit(solution)/shard_map/while/body/eval_jaxpr/psum | solution.py:28
  1835.2 77.2 %all-reduce.9.cloned.1.call-start = ((), (), s32[]{:S(2)}) async-start(), calls=%async_computation.24 | async-start | bytes 589824 | tf_op jit(solution)/shard_map/while/body/eval_jaxpr/psum | solution.py:28
  1914.0 77.2 %all-reduce.9.cloned.1.call-start = ((), (), s32[]{:S(2)}) async-start(), calls=%async_computation.24 | async-start | bytes 589824 | tf_op jit(solution)/shard_map/while/body/eval_jaxpr/psum | solution.py:28
  1992.9 77.2 %all-reduce.9.cloned.1.call-start = ((), (), s32[]{:S(2)}) async-start(), calls=%async_computation.24 | async-start | bytes 589824 | tf_op jit(solution)/shard_map/while/body/eval_jaxpr/psum | solution.py:28
  2099.8 73.5 %reduce-scatter.13.cloned.1.call-start = ((), (), s32[]{:S(2)}) async-start(), calls=%async_computation.9 | async-start | bytes 2949120 | tf_op jit(solution)/shard_map/reduce_scatter | solution.py:131
  2176.0 69.9 %reduce-scatter.15.cloned.1.call-start = ((), (), s32[]{:S(2)}) async-start(), calls=%async_computation.11 | async-start | bytes 2949120 | tf_op jit(solution)/shard_map/reduce_scatter | solution.py:131
  2402.7 79.4 %reduce-scatter.21.cloned.1.call-start = ((), (), s32[]{:S(2)}) async-start(), calls=%async_computation.17 | async-start | bytes 2949120 | tf_op jit(solution)/shard_map/reduce_scatter | solution.py:131
  2490.3 97.4 %reduce-scatter.23.cloned.1.call-start = ((), (), s32[]{:S(2)}) async-start(), calls=%async_computation.19 | async-start | bytes 2949120 | tf_op jit(solution)/shard_map/reduce_scatter | solution.py:131
  2620.2 146.9 %all-reduce.7.cloned.1.call-start = ((), (), s32[]{:S(2)}) async-start(), calls=%async_computation.21 | async-start | bytes 294912 | tf_op jit(solution)/shard_map/psum | solution.py:306
  2620.9 719.2 %all-reduce.5.cloned.1.call-start = ((), (), s32[]{:S(2)}) async-start(), calls=%async_computation.20 | async-start | bytes 37748736 | tf_op jit(solution)/shard_map/psum | solution.py:304
  (147 other events, 16476.6 us)
Sparse Core Ops, SparseCore 0:
  24.7 73.5 all-reduce.8
  107.1 69.9 all-reduce.8
  186.0 69.9 all-reduce.8
  264.8 69.9 all-reduce.8
  343.7 69.9 all-reduce.8
  422.6 69.9 all-reduce.8
  501.5 69.9 all-reduce.8
  580.3 69.9 all-reduce.8
  659.2 69.9 all-reduce.8
  738.1 69.9 all-reduce.8
  817.0 69.9 all-reduce.8
  895.8 69.9 all-reduce.8
  974.7 69.9 all-reduce.8
  1053.6 69.9 all-reduce.8
  1132.4 69.9 all-reduce.8
  1211.3 69.9 all-reduce.8
  1290.2 69.9 all-reduce.8
  1369.1 69.9 all-reduce.8
  1448.0 69.9 all-reduce.8
  1526.9 69.9 all-reduce.8
  1605.7 69.9 all-reduce.8
  1684.6 69.9 all-reduce.8
  1763.5 69.9 all-reduce.8
  1842.4 69.9 all-reduce.8
  1921.2 69.9 all-reduce.8
  2000.1 69.9 all-reduce.8
Sparse Core Ops, SparseCore 1:
  2099.9 23.0 all-gather.7
  2140.3 32.9 reduce-scatter.12
  2176.0 23.9 all-gather.9
  2212.9 32.9 reduce-scatter.14
  2249.8 23.9 all-gather.11
  2283.9 33.0 reduce-scatter.16
  2326.2 23.9 all-gather.13
  2362.3 32.9 reduce-scatter.18
  2402.8 23.9 all-gather.15
  2449.1 33.0 reduce-scatter.20
  2490.4 23.9 all-gather.17
  2554.7 33.0 reduce-scatter.22
  2596.2 19.7 reduce-scatter.24
  2620.2 20.7 reduce-scatter.26
  2646.6 120.4 all-reduce.6
  2771.1 568.9 all-reduce.4
where the time goes:
time: 3450 us; the launch traced here: 3430 us
  waiting for transfers between devices  2770 us (80%)
  local copies, waits for them, and re-layouts  219 us (6%)
  matrix products  128 us (4%)
  loops' own time  119 us (3%)
  other arithmetic  89.9 us (3%)
  blocking collectives  76.2 us (2%)
    psum x26, waiting for transfers between devices, broadcast(): return lax.psum(jnp.where(mine, array, jnp.zeros_like(array)), axis)  1830 us
    psum x1, waiting for transfers between devices, body(): summed = lax.psum(grads, 'dp')  571 us
    all_gather x6, waiting for transfers between devices, spread(): return lax.all_gather(values, 'mp', axis=1, tiled=True)  137 us
    reduce_scatter x6, waiting for transfers between devices, collect(): lax.psum_scatter(values.astype(jnp.bfloat16), 'mp', scatter_dimension=1,...  130 us
    another operation x1, loops' own time, body(): _, fetched = lax.scan(fetch_one, 0, jnp.arange(UNITS))  118 us
    dot_general x55, matrix products, matmul(): return jnp.einsum(form, left, right, preferred_element_type=single)  107 us
    psum x1, waiting for transfers between devices, body(): lax.psum((jnp.stack([grad_in_proj, grad_out_proj]), loss_local), ('dp', '...  73.2 us
  transfers between devices with their start and end apart: 42, of which 42 were waited for; matrix products, arithmetic and copies ran while one was open for 3% of the time, Pallas kernels for 0%

commit v1 on v0

--- a/solution.py
+++ b/solution.py
@@ -301,7 +301,11 @@
     local_ids = lax.axis_index("dp") * slots + jnp.arange(slots)
     pick = (unit_slot[None, :] == local_ids[:, None]).astype(single)
     live_slot = jnp.sum(pick, axis=1) > 0.5
-    summed = lax.psum(grads, "dp")
+    axis_len = lax.axis_size("dp")
+    summed = grads
+    for q in [[(k, k ^ no) for k in range(axis_len)] for no in (1, 2, 4, 8, 16) if no < axis_len]:
+        passed = lax.ppermute(summed, "dp", q)
+        summed = summed + passed
     owned = jnp.einsum("su,ude->sde", pick, summed, precision=highest)
     latent_grad, loss_sum = lax.psum(
         (jnp.stack([grad_in_proj, grad_out_proj]), loss_local), ("dp", "mp")

time: 3450 us -> 4190 us (1.21)
  waiting for transfers between devices: 2770 us -> 3520 us
  local copies, waits for them, and re-layouts: 219 us -> 166 us
    ppermute x0 -> x3, waiting for transfers between devices: none -> 659 us  [body(): passed = lax.ppermute(summed, 'dp', q)]
    psum x1, waiting for transfers between devices: 73.2 us -> 727 us  [body(): lax.psum((jnp.stack([grad_in_proj, grad_out_proj]), loss_local), ('dp', '...]
    psum x1 -> x0, waiting for transfers between devices: 571 us -> none  [body(): summed = lax.psum(grads, 'dp')]
    concatenate x1 -> x0, local copies, waits for them, and re-layouts: 46 us -> none  [body(): jnp.concatenate([columns(grad_w_attn, 3), grad_w_self_out[None], grad_w_c...]
  transfers between devices with their start and end apart: 42 -> 44, of which waited for: 42 -> 43; matrix products, arithmetic and copies ran while one was open for 3% -> 1% of each run, Pallas kernels for 0% -> 0%
where the time goes in v1:
time: 4190 us; the launch traced here: 4170 us
  waiting for transfers between devices  3520 us (84%)
  local copies, waits for them, and re-layouts  166 us (4%)
  matrix products  137 us (3%)
  other arithmetic  125 us (3%)
  loops' own time  119 us (3%)
  blocking collectives  78.9 us (2%)
    psum x26, waiting for transfers between devices, broadcast(): return lax.psum(jnp.where(mine, array, jnp.zeros_like(array)), axis)  1830 us
    psum x1, waiting for transfers between devices, body(): lax.psum((jnp.stack([grad_in_proj, grad_out_proj]), loss_local), ('dp', '...  727 us
    ppermute x3, waiting for transfers between devices, body(): passed = lax.ppermute(summed, 'dp', q)  659 us
    all_gather x6, waiting for transfers between devices, spread(): return lax.all_gather(values, 'mp', axis=1, tiled=True)  136 us
    reduce_scatter x6, waiting for transfers between devices, collect(): lax.psum_scatter(values.astype(jnp.bfloat16), 'mp', scatter_dimension=1,...  135 us
    another operation x1, loops' own time, body(): _, fetched = lax.scan(fetch_one, 0, jnp.arange(UNITS))  118 us
    dot_general x55, matrix products, matmul(): return jnp.einsum(form, left, right, preferred_element_type=single)  111 us
  transfers between devices with their start and end apart: 44, of which 43 were waited for; matrix products, arithmetic and copies ran while one was open for 1% of the time, Pallas kernels for 0%

profile of v1, /device:TPU:0, one launch (start us, length us, event | category | flops | bytes accessed | tf_op | source)
XLA Modules:
  0.0 4173.2 jit_solution(1273941460478023210)
XLA Ops:
  17.4 2054.3 %while.62 = (s32[]{:T(128)}, bf16[26,192,768]{2,1,0:T(8,128)(2,1)}, s32[26]{0:T(128)S(1)}, s32[26]{0:T(128)S(1)}, s32[26]{0:T(128)S(1)}, /*index=5*/bf16[5,192,7...) while((s32[]{:T(128)}, bf16[26,192,768]{2,1,0:T(8,128)(2,1)}, ...), condition=%wide.region_5.6_spmd, body=%wide.region_3.5_spmd.sunk | while | flops 294924 | bytes 2949439 | solution.py:164
  24.6 73.7 %all-reduce.6.cloned.1.call-done = bf16[1,192,768]{2,1,0:T(8,128)(2,1)} async-done(((bf16[1,192,768]{2,1,0:T(8,128)(2,1)}), bf16[1,192,768]{2,1,0:T(8,128)(2,1)}) %all-reduce.6.cloned.1.call-update) | async-done | bytes 294928 | tf_op jit(solution)/shard_map/while/body/eval_jaxpr/psum | solution.py:28
  107.0 70.1 %all-reduce.6.cloned.1.call-done = bf16[1,192,768]{2,1,0:T(8,128)(2,1)} async-done(((bf16[1,192,768]{2,1,0:T(8,128)(2,1)}), bf16[1,192,768]{2,1,0:T(8,128)(2,1)}) %all-reduce.6.cloned.1.call-update) | async-done | bytes 294928 | tf_op jit(solution)/shard_map/while/body/eval_jaxpr/psum | solution.py:28
  185.9 70.1 %all-reduce.6.cloned.1.call-done = bf16[1,192,768]{2,1,0:T(8,128)(2,1)} async-done(((bf16[1,192,768]{2,1,0:T(8,128)(2,1)}), bf16[1,192,768]{2,1,0:T(8,128)(2,1)}) %all-reduce.6.cloned.1.call-update) | async-done | bytes 294928 | tf_op jit(solution)/shard_map/while/body/eval_jaxpr/psum | solution.py:28
  264.7 70.1 %all-reduce.6.cloned.1.call-done = bf16[1,192,768]{2,1,0:T(8,128)(2,1)} async-done(((bf16[1,192,768]{2,1,0:T(8,128)(2,1)}), bf16[1,192,768]{2,1,0:T(8,128)(2,1)}) %all-reduce.6.cloned.1.call-update) | async-done | bytes 294928 | tf_op jit(solution)/shard_map/while/body/eval_jaxpr/psum | solution.py:28
  343.6 70.1 %all-reduce.6.cloned.1.call-done = bf16[1,192,768]{2,1,0:T(8,128)(2,1)} async-done(((bf16[1,192,768]{2,1,0:T(8,128)(2,1)}), bf16[1,192,768]{2,1,0:T(8,128)(2,1)}) %all-reduce.6.cloned.1.call-update) | async-done | bytes 294928 | tf_op jit(solution)/shard_map/while/body/eval_jaxpr/psum | solution.py:28
  422.5 70.1 %all-reduce.6.cloned.1.call-done = bf16[1,192,768]{2,1,0:T(8,128)(2,1)} async-done(((bf16[1,192,768]{2,1,0:T(8,128)(2,1)}), bf16[1,192,768]{2,1,0:T(8,128)(2,1)}) %all-reduce.6.cloned.1.call-update) | async-done | bytes 294928 | tf_op jit(solution)/shard_map/while/body/eval_jaxpr/psum | solution.py:28
  501.3 70.1 %all-reduce.6.cloned.1.call-done = bf16[1,192,768]{2,1,0:T(8,128)(2,1)} async-done(((bf16[1,192,768]{2,1,0:T(8,128)(2,1)}), bf16[1,192,768]{2,1,0:T(8,128)(2,1)}) %all-reduce.6.cloned.1.call-update) | async-done | bytes 294928 | tf_op jit(solution)/shard_map/while/body/eval_jaxpr/psum | solution.py:28
  580.2 70.1 %all-reduce.6.cloned.1.call-done = bf16[1,192,768]{2,1,0:T(8,128)(2,1)} async-done(((bf16[1,192,768]{2,1,0:T(8,128)(2,1)}), bf16[1,192,768]{2,1,0:T(8,128)(2,1)}) %all-reduce.6.cloned.1.call-update) | async-done | bytes 294928 | tf_op jit(solution)/shard_map/while/body/eval_jaxpr/psum | solution.py:28
  659.1 70.1 %all-reduce.6.cloned.1.call-done = bf16[1,192,768]{2,1,0:T(8,128)(2,1)} async-done(((bf16[1,192,768]{2,1,0:T(8,128)(2,1)}), bf16[1,192,768]{2,1,0:T(8,128)(2,1)}) %all-reduce.6.cloned.1.call-update) | async-done | bytes 294928 | tf_op jit(solution)/shard_map/while/body/eval_jaxpr/psum | solution.py:28
  737.9 70.1 %all-reduce.6.cloned.1.call-done = bf16[1,192,768]{2,1,0:T(8,128)(2,1)} async-done(((bf16[1,192,768]{2,1,0:T(8,128)(2,1)}), bf16[1,192,768]{2,1,0:T(8,128)(2,1)}) %all-reduce.6.cloned.1.call-update) | async-done | bytes 294928 | tf_op jit(solution)/shard_map/while/body/eval_jaxpr/psum | solution.py:28
  816.8 70.1 %all-reduce.6.cloned.1.call-done = bf16[1,192,768]{2,1,0:T(8,128)(2,1)} async-done(((bf16[1,192,768]{2,1,0:T(8,128)(2,1)}), bf16[1,192,768]{2,1,0:T(8,128)(2,1)}) %all-reduce.6.cloned.1.call-update) | async-done | bytes 294928 | tf_op jit(solution)/shard_map/while/body/eval_jaxpr/psum | solution.py:28
  895.7 70.1 %all-reduce.6.cloned.1.call-done = bf16[1,192,768]{2,1,0:T(8,128)(2,1)} async-done(((bf16[1,192,768]{2,1,0:T(8,128)(2,1)}), bf16[1,192,768]{2,1,0:T(8,128)(2,1)}) %all-reduce.6.cloned.1.call-update) | async-done | bytes 294928 | tf_op jit(solution)/shard_map/while/body/eval_jaxpr/psum | solution.py:28
  974.6 70.1 %all-reduce.6.cloned.1.call-done = bf16[1,192,768]{2,1,0:T(8,128)(2,1)} async-done(((bf16[1,192,768]{2,1,0:T(8,128)(2,1)}), bf16[1,192,768]{2,1,0:T(8,128)(2,1)}) %all-reduce.6.cloned.1.call-update) | async-done | bytes 294928 | tf_op jit(solution)/shard_map/while/body/eval_jaxpr/psum | solution.py:28
  1053.5 70.1 %all-reduce.6.cloned.1.call-done = bf16[1,192,768]{2,1,0:T(8,128)(2,1)} async-done(((bf16[1,192,768]{2,1,0:T(8,128)(2,1)}), bf16[1,192,768]{2,1,0:T(8,128)(2,1)}) %all-reduce.6.cloned.1.call-update) | async-done | bytes 294928 | tf_op jit(solution)/shard_map/while/body/eval_jaxpr/psum | solution.py:28
  1132.3 70.1 %all-reduce.6.cloned.1.call-done = bf16[1,192,768]{2,1,0:T(8,128)(2,1)} async-done(((bf16[1,192,768]{2,1,0:T(8,128)(2,1)}), bf16[1,192,768]{2,1,0:T(8,128)(2,1)}) %all-reduce.6.cloned.1.call-update) | async-done | bytes 294928 | tf_op jit(solution)/shard_map/while/body/eval_jaxpr/psum | solution.py:28
  1211.2 70.1 %all-reduce.6.cloned.1.call-done = bf16[1,192,768]{2,1,0:T(8,128)(2,1)} async-done(((bf16[1,192,768]{2,1,0:T(8,128)(2,1)}), bf16[1,192,768]{2,1,0:T(8,128)(2,1)}) %all-reduce.6.cloned.1.call-update) | async-done | bytes 294928 | tf_op jit(solution)/shard_map/while/body/eval_jaxpr/psum | solution.py:28
  1290.1 70.1 %all-reduce.6.cloned.1.call-done = bf16[1,192,768]{2,1,0:T(8,128)(2,1)} async-done(((bf16[1,192,768]{2,1,0:T(8,128)(2,1)}), bf16[1,192,768]{2,1,0:T(8,128)(2,1)}) %all-reduce.6.cloned.1.call-update) | async-done | bytes 294928 | tf_op jit(solution)/shard_map/while/body/eval_jaxpr/psum | solution.py:28
  1368.9 70.1 %all-reduce.6.cloned.1.call-done = bf16[1,192,768]{2,1,0:T(8,128)(2,1)} async-done(((bf16[1,192,768]{2,1,0:T(8,128)(2,1)}), bf16[1,192,768]{2,1,0:T(8,128)(2,1)}) %all-reduce.6.cloned.1.call-update) | async-done | bytes 294928 | tf_op jit(solution)/shard_map/while/body/eval_jaxpr/psum | solution.py:28
  1447.8 70.1 %all-reduce.6.cloned.1.call-done = bf16[1,192,768]{2,1,0:T(8,128)(2,1)} async-done(((bf16[1,192,768]{2,1,0:T(8,128)(2,1)}), bf16[1,192,768]{2,1,0:T(8,128)(2,1)}) %all-reduce.6.cloned.1.call-update) | async-done | bytes 294928 | tf_op jit(solution)/shard_map/while/body/eval_jaxpr/psum | solution.py:28
  1526.7 70.1 %all-reduce.6.cloned.1.call-done = bf16[1,192,768]{2,1,0:T(8,128)(2,1)} async-done(((bf16[1,192,768]{2,1,0:T(8,128)(2,1)}), bf16[1,192,768]{2,1,0:T(8,128)(2,1)}) %all-reduce.6.cloned.1.call-update) | async-done | bytes 294928 | tf_op jit(solution)/shard_map/while/body/eval_jaxpr/psum | solution.py:28
  1605.6 70.1 %all-reduce.6.cloned.1.call-done = bf16[1,192,768]{2,1,0:T(8,128)(2,1)} async-done(((bf16[1,192,768]{2,1,0:T(8,128)(2,1)}), bf16[1,192,768]{2,1,0:T(8,128)(2,1)}) %all-reduce.6.cloned.1.call-update) | async-done | bytes 294928 | tf_op jit(solution)/shard_map/while/body/eval_jaxpr/psum | solution.py:28
  1684.4 70.1 %all-reduce.6.cloned.1.call-done = bf16[1,192,768]{2,1,0:T(8,128)(2,1)} async-done(((bf16[1,192,768]{2,1,0:T(8,128)(2,1)}), bf16[1,192,768]{2,1,0:T(8,128)(2,1)}) %all-reduce.6.cloned.1.call-update) | async-done | bytes 294928 | tf_op jit(solution)/shard_map/while/body/eval_jaxpr/psum | solution.py:28
  1763.3 70.1 %all-reduce.6.cloned.1.call-done = bf16[1,192,768]{2,1,0:T(8,128)(2,1)} async-done(((bf16[1,192,768]{2,1,0:T(8,128)(2,1)}), bf16[1,192,768]{2,1,0:T(8,128)(2,1)}) %all-reduce.6.cloned.1.call-update) | async-done | bytes 294928 | tf_op jit(solution)/shard_map/while/body/eval_jaxpr/psum | solution.py:28
  1842.2 70.1 %all-reduce.6.cloned.1.call-done = bf16[1,192,768]{2,1,0:T(8,128)(2,1)} async-done(((bf16[1,192,768]{2,1,0:T(8,128)(2,1)}), bf16[1,192,768]{2,1,0:T(8,128)(2,1)}) %all-reduce.6.cloned.1.call-update) | async-done | bytes 294928 | tf_op jit(solution)/shard_map/while/body/eval_jaxpr/psum | solution.py:28
  1921.0 70.1 %all-reduce.6.cloned.1.call-done = bf16[1,192,768]{2,1,0:T(8,128)(2,1)} async-done(((bf16[1,192,768]{2,1,0:T(8,128)(2,1)}), bf16[1,192,768]{2,1,0:T(8,128)(2,1)}) %all-reduce.6.cloned.1.call-update) | async-done | bytes 294928 | tf_op jit(solution)/shard_map/while/body/eval_jaxpr/psum | solution.py:28
  1999.9 70.1 %all-reduce.6.cloned.1.call-done = bf16[1,192,768]{2,1,0:T(8,128)(2,1)} async-done(((bf16[1,192,768]{2,1,0:T(8,128)(2,1)}), bf16[1,192,768]{2,1,0:T(8,128)(2,1)}) %all-reduce.6.cloned.1.call-update) | async-done | bytes 294928 | tf_op jit(solution)/shard_map/while/body/eval_jaxpr/psum | solution.py:28
  2362.0 33.0 reduce-scatter.19.cloned.1.call-done
  2643.8 329.8 %collective-permute-done = f32[26,192,768]{2,1,0:T(8,128)} collective-permute-done((f32[26,192,768]{2,1,0:T(8,128)}, f32[26,192,768]{2,1,0:T(8,128)}, u32[]{:S(2)}, u32[]{:S(2)}) %collective-permute-start) | collective-permute-done | bytes 15335456 | tf_op jit(solution)/shard_map/ppermute | solution.py:307
  2985.8 328.7 %collective-permute-done.1 = f32[26,192,768]{2,1,0:T(8,128)} collective-permute-done((f32[26,192,768]{2,1,0:T(8,128)S(1)}, f32[26,192,768]{2,1,0:T(8,128)}, u32[]{:S(2)}, u32[]{:S(2)}) %collective-permute-start.1) | collective-permute-done | bytes 15335456 | tf_op jit(solution)/shard_map/ppermute | solution.py:307
  3337.3 726.7 %all-reduce.4.cloned.1.call-done = f32[2,20,768]{2,1,0:T(8,128)} async-done(((f32[2,20,768]{2,1,0:T(8,128)}), f32[2,20,768]{2,1,0:T(8,128)}) %all-reduce.4.cloned.1.call-update) | async-done | bytes 122896 | tf_op jit(solution)/shard_map/psum | solution.py:310
  4091.9 42.7 %all-reduce = (f32[]{:T(128)}, f32[]{:T(128)}) all-reduce(f32[]{:T(128)} %get-tuple-element.410, f32[]{:T(128)} %get-tuple-element.412), channel_id=1, replica_groups=mesh['dp'=8,'mp'=4] {'dp','mp'}, use_global_device_ids=true, to_apply=%region_53.54 | all-reduce | flops 2 | bytes 16 | tf_op jit(solution)/shard_map/psum | solution.py:313
  (707 shorter events, 803.7 us)
Async XLA Ops:
  17.4 80.8 %all-reduce.6.cloned.1.call-start = ((), (), s32[]{:S(2)}) async-start(), calls=%async_computation.23 | async-start | bytes 589824 | tf_op jit(solution)/shard_map/while/body/eval_jaxpr/psum | solution.py:28
  100.0 77.2 %all-reduce.6.cloned.1.call-start = ((), (), s32[]{:S(2)}) async-start(), calls=%async_computation.23 | async-start | bytes 589824 | tf_op jit(solution)/shard_map/while/body/eval_jaxpr/psum | solution.py:28
  178.8 77.2 %all-reduce.6.cloned.1.call-start = ((), (), s32[]{:S(2)}) async-start(), calls=%async_computation.23 | async-start | bytes 589824 | tf_op jit(solution)/shard_map/while/body/eval_jaxpr/psum | solution.py:28
  257.7 77.2 %all-reduce.6.cloned.1.call-start = ((), (), s32[]{:S(2)}) async-start(), calls=%async_computation.23 | async-start | bytes 589824 | tf_op jit(solution)/shard_map/while/body/eval_jaxpr/psum | solution.py:28
  336.5 77.2 %all-reduce.6.cloned.1.call-start = ((), (), s32[]{:S(2)}) async-start(), calls=%async_computation.23 | async-start | bytes 589824 | tf_op jit(solution)/shard_map/while/body/eval_jaxpr/psum | solution.py:28
  415.4 77.2 %all-reduce.6.cloned.1.call-start = ((), (), s32[]{:S(2)}) async-start(), calls=%async_computation.23 | async-start | bytes 589824 | tf_op jit(solution)/shard_map/while/body/eval_jaxpr/psum | solution.py:28
  494.3 77.2 %all-reduce.6.cloned.1.call-start = ((), (), s32[]{:S(2)}) async-start(), calls=%async_computation.23 | async-start | bytes 589824 | tf_op jit(solution)/shard_map/while/body/eval_jaxpr/psum | solution.py:28
  573.1 77.2 %all-reduce.6.cloned.1.call-start = ((), (), s32[]{:S(2)}) async-start(), calls=%async_computation.23 | async-start | bytes 589824 | tf_op jit(solution)/shard_map/while/body/eval_jaxpr/psum | solution.py:28
  652.0 77.2 %all-reduce.6.cloned.1.call-start = ((), (), s32[]{:S(2)}) async-start(), calls=%async_computation.23 | async-start | bytes 589824 | tf_op jit(solution)/shard_map/while/body/eval_jaxpr/psum | solution.py:28
  730.9 77.2 %all-reduce.6.cloned.1.call-start = ((), (), s32[]{:S(2)}) async-start(), calls=%async_computation.23 | async-start | bytes 589824 | tf_op jit(solution)/shard_map/while/body/eval_jaxpr/psum | solution.py:28
  809.8 77.2 %all-reduce.6.cloned.1.call-start = ((), (), s32[]{:S(2)}) async-start(), calls=%async_computation.23 | async-start | bytes 589824 | tf_op jit(solution)/shard_map/while/body/eval_jaxpr/psum | solution.py:28
  888.6 77.2 %all-reduce.6.cloned.1.call-start = ((), (), s32[]{:S(2)}) async-start(), calls=%async_computation.23 | async-start | bytes 589824 | tf_op jit(solution)/shard_map/while/body/eval_jaxpr/psum | solution.py:28
  967.5 77.2 %all-reduce.6.cloned.1.call-start = ((), (), s32[]{:S(2)}) async-start(), calls=%async_computation.23 | async-start | bytes 589824 | tf_op jit(solution)/shard_map/while/body/eval_jaxpr/psum | solution.py:28
  1046.4 77.2 %all-reduce.6.cloned.1.call-start = ((), (), s32[]{:S(2)}) async-start(), calls=%async_computation.23 | async-start | bytes 589824 | tf_op jit(solution)/shard_map/while/body/eval_jaxpr/psum | solution.py:28
  1125.3 77.2 %all-reduce.6.cloned.1.call-start = ((), (), s32[]{:S(2)}) async-start(), calls=%async_computation.23 | async-start | bytes 589824 | tf_op jit(solution)/shard_map/while/body/eval_jaxpr/psum | solution.py:28
  1204.1 77.2 %all-reduce.6.cloned.1.call-start = ((), (), s32[]{:S(2)}) async-start(), calls=%async_computation.23 | async-start | bytes 589824 | tf_op jit(solution)/shard_map/while/body/eval_jaxpr/psum | solution.py:28
  1283.0 77.2 %all-reduce.6.cloned.1.call-start = ((), (), s32[]{:S(2)}) async-start(), calls=%async_computation.23 | async-start | bytes 589824 | tf_op jit(solution)/shard_map/while/body/eval_jaxpr/psum | solution.py:28
  1361.9 77.2 %all-reduce.6.cloned.1.call-start = ((), (), s32[]{:S(2)}) async-start(), calls=%async_computation.23 | async-start | bytes 589824 | tf_op jit(solution)/shard_map/while/body/eval_jaxpr/psum | solution.py:28
  1440.7 77.2 %all-reduce.6.cloned.1.call-start = ((), (), s32[]{:S(2)}) async-start(), calls=%async_computation.23 | async-start | bytes 589824 | tf_op jit(solution)/shard_map/while/body/eval_jaxpr/psum | solution.py:28
  1519.6 77.2 %all-reduce.6.cloned.1.call-start = ((), (), s32[]{:S(2)}) async-start(), calls=%async_computation.23 | async-start | bytes 589824 | tf_op jit(solution)/shard_map/while/body/eval_jaxpr/psum | solution.py:28
  1598.5 77.2 %all-reduce.6.cloned.1.call-start = ((), (), s32[]{:S(2)}) async-start(), calls=%async_computation.23 | async-start | bytes 589824 | tf_op jit(solution)/shard_map/while/body/eval_jaxpr/psum | solution.py:28
  1677.4 77.2 %all-reduce.6.cloned.1.call-start = ((), (), s32[]{:S(2)}) async-start(), calls=%async_computation.23 | async-start | bytes 589824 | tf_op jit(solution)/shard_map/while/body/eval_jaxpr/psum | solution.py:28
  1756.2 77.2 %all-reduce.6.cloned.1.call-start = ((), (), s32[]{:S(2)}) async-start(), calls=%async_computation.23 | async-start | bytes 589824 | tf_op jit(solution)/shard_map/while/body/eval_jaxpr/psum | solution.py:28
  1835.1 77.2 %all-reduce.6.cloned.1.call-start = ((), (), s32[]{:S(2)}) async-start(), calls=%async_computation.23 | async-start | bytes 589824 | tf_op jit(solution)/shard_map/while/body/eval_jaxpr/psum | solution.py:28
  1914.0 77.2 %all-reduce.6.cloned.1.call-start = ((), (), s32[]{:S(2)}) async-start(), calls=%async_computation.23 | async-start | bytes 589824 | tf_op jit(solution)/shard_map/while/body/eval_jaxpr/psum | solution.py:28
  1992.9 77.2 %all-reduce.6.cloned.1.call-start = ((), (), s32[]{:S(2)}) async-start(), calls=%async_computation.23 | async-start | bytes 589824 | tf_op jit(solution)/shard_map/while/body/eval_jaxpr/psum | solution.py:28
  2402.3 79.4 %reduce-scatter.21.cloned.1.call-start = ((), (), s32[]{:S(2)}) async-start(), calls=%async_computation.17 | async-start | bytes 2949120 | tf_op jit(solution)/shard_map/reduce_scatter | solution.py:131
  2489.8 97.1 %reduce-scatter.23.cloned.1.call-start = ((), (), s32[]{:S(2)}) async-start(), calls=%async_computation.19 | async-start | bytes 2949120 | tf_op jit(solution)/shard_map/reduce_scatter | solution.py:131
  2618.2 1445.8 %all-reduce.4.cloned.1.call-start = ((), (), s32[]{:S(2)}) async-start(), calls=%async_computation.20 | async-start | bytes 294912 | tf_op jit(solution)/shard_map/psum | solution.py:310
  2642.3 331.3 %collective-permute-start = (f32[26,192,768]{2,1,0:T(8,128)}, f32[26,192,768]{2,1,0:T(8,128)}, u32[]{:S(2)}, u32[]{:S(2)}) collective-permute-start(f32[26,192,768]{2,1,0:T(8,128)} %bitcast.129), channel_id=1, source_target_pairs={{0,4},{4,0},{8,12},{12,8},{16,20},{20,16},{24,28},{28,24},{1,5},{5... | collective-permute-start | bytes 46006280 | tf_op jit(solution)/shard_map/ppermute | solution.py:307
  2984.2 330.2 %collective-permute-start.1 = (f32[26,192,768]{2,1,0:T(8,128)S(1)}, f32[26,192,768]{2,1,0:T(8,128)}, u32[]{:S(2)}, u32[]{:S(2)}) collective-permute-start(f32[26,192,768]{2,1,0:T(8,128)S(1)} %bitcast_add_fusion), channel_id=1, source_target_pairs={{0,8},{4,12},{8,0},{12,4},{16,24},{20,28},{24,16},{28,20},{1,9},{5... | collective-permute-start | bytes 46006280 | tf_op jit(solution)/shard_map/ppermute | solution.py:307
  3326.1 739.5 %collective-permute-start.2 = (f32[26,192,768]{2,1,0:T(8,128)}, f32[26,192,768]{2,1,0:T(8,128)}, u32[]{:S(2)}, u32[]{:S(2)}) collective-permute-start(f32[26,192,768]{2,1,0:T(8,128)} %add.297), channel_id=1, source_target_pairs={{0,16},{4,20},{8,24},{12,28},{16,0},{20,4},{24,8},{28,12},{1,17},{... | collective-permute-start | bytes 46006280 | tf_op jit(solution)/shard_map/ppermute | solution.py:307
  (148 other events, 17126.5 us)
Sparse Core Ops, SparseCore 0:
  24.7 73.5 all-reduce.5
  107.1 69.9 all-reduce.5
  186.0 69.9 all-reduce.5
  264.9 69.9 all-reduce.5
  343.7 69.9 all-reduce.5
  422.6 69.9 all-reduce.5
  501.5 69.9 all-reduce.5
  580.3 69.9 all-reduce.5
  659.2 69.9 all-reduce.5
  738.1 69.9 all-reduce.5
  816.9 69.9 all-reduce.5
  895.8 69.9 all-reduce.5
  974.7 69.9 all-reduce.5
  1053.6 69.9 all-reduce.5
  1132.5 69.9 all-reduce.5
  1211.3 69.9 all-reduce.5
  1290.2 69.9 all-reduce.5
  1369.1 69.9 all-reduce.5
  1447.9 69.9 all-reduce.5
  1526.8 69.9 all-reduce.5
  1605.7 69.9 all-reduce.5
  1684.5 69.9 all-reduce.5
  1763.4 69.9 all-reduce.5
  1842.3 69.9 all-reduce.5
  1921.2 69.9 all-reduce.5
  2000.0 69.9 all-reduce.5
Sparse Core Ops, SparseCore 1:
  2099.8 23.0 all-gather.7
  2140.1 33.0 reduce-scatter.12
  2175.9 23.9 all-gather.9
  2212.7 33.0 reduce-scatter.14
  2249.6 23.9 all-gather.11
  2283.7 32.9 reduce-scatter.16
  2325.9 23.9 all-gather.13
  2362.0 33.0 reduce-scatter.18
  2402.4 23.9 all-gather.15
  2448.7 32.9 reduce-scatter.20
  2489.9 23.9 all-gather.17
  2553.9 33.0 reduce-scatter.22
  2593.9 19.7 reduce-scatter.24
  2618.3 20.7 reduce-scatter.26
  3336.0 727.9 all-reduce.3
